TPU v7x, 32 devices: a whole 2x2x4 slice. The times are simulated.
32 devices in a mesh: groups: 2 (over x), dp: 16 (over z, y, core).
Axes of the slice: x: 2, y: 2, z: 4, core: 2. Of those that a mesh axis runs over, the one named last changes fastest.
Arguments:
- tokens: bfloat16 [16384, 4096], P(('groups', 'dp')), parts along dimension 0, may hold values from -6 to 6
- base_weight: bfloat16 [4096, 1024], P('dp'), may hold values from -0.09375 to 0.09375
- shrink_store: bfloat16 [32, 4096, 64], P('dp'), may hold values from -0.09375 to 0.09375
- expand_store: bfloat16 [32, 64, 1024], P('dp'), may hold values from -0.75 to 0.75
- request_adapter: int32 [64], P('groups'), parts along dimension 0, may hold values from 0 to 31
- adapter_slot: int32 [32], replicated, may hold values from 0 to 31, each once
Outputs:
- mixed: bfloat16 [16384, 1024], P(('groups', 'dp')), parts along dimension 0
There are 2 independent parts, one for each index of `groups`. A program takes and returns all parts, laid end to end along the dimension named above; an argument that names none is the same for every part. Nothing has to cross between parts.
Inputs may be any that keep to these rules, and one draw needn't show every extreme that they name: `request_adapter`: each request names one of the 32 adapters; some adapters are named by many requests. `adapter_slot`: each store slot holds exactly one adapter.
All inputs are finite; a program needn't handle non-finite values.
Results may differ from a plain program's by a relative error of at most 0.0052.
Values may be sent and summed in bfloat16 or wider, within the bound.
A program may use at most 128 MiB of HBM per device.

v0:
```python
import jax
import jax.numpy as jnp
from jax import lax
from jax.sharding import PartitionSpec as P


def shards(tokens, base_weight, shrink_store, expand_store, request_adapter, adapter_slot):
    tok_rows = tokens.shape[0]
    num_requests = request_adapter.shape[0]
    num_adapters = adapter_slot.shape[0]
    dp_count = lax.axis_size("dp")
    seg_len = tok_rows * dp_count // num_requests
    base_out = jnp.dot(
        tokens,
        lax.all_gather(base_weight, "dp", axis=0, tiled=True),
        preferred_element_type=jnp.float32,
    )
    matches = request_adapter[:, None] == jnp.arange(num_adapters, dtype=jnp.int32)[None, :]
    slot_ids = jnp.sum(jnp.where(matches, adapter_slot[None, :], 0), axis=1)
    shrink_blocks = lax.all_to_all(shrink_store, "dp", split_axis=1, concat_axis=0, tiled=True)
    expand_blocks = lax.all_to_all(expand_store, "dp", split_axis=2, concat_axis=0, tiled=True)
    picked = jnp.take(shrink_blocks, slot_ids, axis=0)
    picked_up = jnp.take(expand_blocks, slot_ids, axis=0)
    token_blocks = lax.all_to_all(tokens, "dp", split_axis=1, concat_axis=0, tiled=True)
    grouped = token_blocks.reshape(num_requests, seg_len, token_blocks.shape[1])
    partial_value = jnp.einsum("qsd,qdr->qsr", grouped, picked, preferred_element_type=jnp.float32)
    shrunk = lax.psum(partial_value, "dp").astype(jnp.bfloat16)
    term_blocks = jnp.einsum(
        "qsr,qrc->qsc", shrunk, picked_up, preferred_element_type=jnp.float32
    ).astype(jnp.bfloat16)
    term_blocks = term_blocks.reshape(num_requests * seg_len, expand_blocks.shape[2])
    low_rank = lax.all_to_all(term_blocks, "dp", split_axis=0, concat_axis=1, tiled=True)
    return (base_out + low_rank.astype(jnp.float32)).astype(jnp.bfloat16)


def solution(mesh):
    return jax.shard_map(
        shards,
        mesh=mesh,
        in_specs=(
            P(("groups", "dp"), None),
            P("dp", None),
            P("dp", None, None),
            P("dp", None, None),
            P("groups"),
            P(),
        ),
        out_specs=P(("groups", "dp"), None),
        check_vma=False,
    )
```

profile of v0, /device:TPU:0, one launch (start us, length us, event | category | flops | bytes accessed | tf_op | source)
XLA Modules:
  0.0 323.6 jit_solution(6188067339377616127)
XLA Ops:
  6.5 0.7 all-gather.2.cloned.1.call-update
  7.3 1.3 copy.36
  8.5 1.1 reshape.54
  9.7 7.4 %all-to-all-start.2 = ((bf16[16,2,4096]{2,1,0:T(2,128)(2,1)}), bf16[16,2,4096]{2,1,0:T(2,128)(2,1)S(1)}, u32[]{:S(2)}, u32[]{:S(2)}) async-start(bf16[16,2,4096]{2,1,0:T(2,128)(2,1)} %reshape.54), calls=%async_computation.2 | async-start | bytes 524288 | tf_op jit(solution)/shard_map/all_to_all | solution.py:21
  17.1 5.1 %copy.31 = bf16[2,4096,64]{2,0,1:T(2,128)(2,1)S(1)} copy(bf16[2,4096,64]{1,2,0:T(8,128)(2,1)} %param.8) | data formatting | bytes 2097152 | tf_op args[2]
  22.2 2.2 reshape.52
  24.4 4.0 %all-to-all-done.2 = bf16[16,2,4096]{2,1,0:T(2,128)(2,1)S(1)} async-done(((bf16[16,2,4096]{2,1,0:T(2,128)(2,1)}), bf16[16,2,4096]{2,1,0:T(2,128)(2,1)S(1)}, u32[]{:S(2)}, u32[]{:S(2)}) %all-to-all-start.2) | async-done | bytes 262176 | tf_op jit(solution)/shard_map/all_to_all | solution.py:21
  28.4 7.0 %all-to-all-start = ((bf16[16,2,16384]{2,1,0:T(2,128)(2,1)}), bf16[16,2,16384]{2,1,0:T(2,128)(2,1)S(1)}, u32[]{:S(2)}, u32[]{:S(2)}) async-start(bf16[16,2,16384]{2,1,0:T(2,128)(2,1)} %reshape.52), calls=%async_computation | async-start | bytes 2097152 | tf_op jit(solution)/shard_map/all_to_all | solution.py:20
  35.5 6.5 %copy.34 = bf16[512,4096]{0,1:T(8,128)(2,1)} copy(bf16[512,4096]{1,0:T(8,128)(2,1)} %param.6) | data formatting | bytes 8388608 | tf_op args[0]
  42.0 26.4 %all-to-all-done = bf16[16,2,16384]{2,1,0:T(2,128)(2,1)S(1)} async-done(((bf16[16,2,16384]{2,1,0:T(2,128)(2,1)}), bf16[16,2,16384]{2,1,0:T(2,128)(2,1)S(1)}, u32[]{:S(2)}, u32[]{:S(2)}) %all-to-all-start) | async-done | bytes 1048608 | tf_op jit(solution)/shard_map/all_to_all | solution.py:20
  68.4 18.6 %all-to-all-start.1 = ((bf16[512,16,256]{0,2,1:T(8,128)(2,1)}), bf16[512,16,256]{0,2,1:T(8,128)(2,1)}, u32[]{:S(2)}, u32[]{:S(2)}) async-start(bf16[512,16,256]{0,2,1:T(8,128)(2,1)} %bitcast.32), calls=%async_computation.1 | async-start | bytes 8388608 | tf_op jit(solution)/shard_map/all_to_all | solution.py:24
  88.0 1.4 gather_fusion.1
  89.4 1.3 reshape.53
  90.8 1.2 copy.45
  92.0 0.6 gather_fusion
  92.6 81.3 %all-to-all-done.1 = bf16[512,16,256]{0,2,1:T(8,128)(2,1)} async-done(((bf16[512,16,256]{0,2,1:T(8,128)(2,1)}), bf16[512,16,256]{0,2,1:T(8,128)(2,1)}, u32[]{:S(2)}, u32[]{:S(2)}) %all-to-all-start.1) | async-done | bytes 4194336 | tf_op jit(solution)/shard_map/all_to_all | solution.py:24
  173.9 6.4 %copy.35 = bf16[16,512,256]{2,1,0:T(8,128)(2,1)} copy(bf16[16,512,256]{1,2,0:T(8,128)(2,1)} %bitcast.7) | data formatting | bytes 8388608 | tf_op jit(solution)/shard_map/all_to_all | solution.py:24
  180.3 3.6 %convolution_bitcast_fusion = f32[32,256,64]{1,2,0:T(8,128)S(1)} fusion(bf16[32,256,256]{2,1,0:T(8,128)(2,1)} %bitcast.33, bf16[32,256,64]{1,2,0:T(8,128)(2,1)S(1)} %gather_fusion, pred[32]{0:T(512)(128)(4,1)S(1)} %compare_and_fusion), kind=kOutput, calls=%fused_computation.3 | convolution fusion | flops 268959744 | bytes 7340064 | tf_op jit(solution)/shard_map/qsd,qdr->qsr/dot_general | solution.py:26
  183.9 89.3 %all-reduce.1 = bf16[32,256,64]{1,2,0:T(8,128)(2,1)S(1)} all-reduce(f32[32,256,64]{1,2,0:T(8,128)S(1)} %convolution_bitcast_fusion), channel_id=1, replica_groups=mesh['groups'=2,'dp'=16] {'dp'}, use_global_device_ids=true, to_apply=%region_1.2 | all-reduce | flops 524288 | bytes 3145728 | tf_op jit(solution)/shard_map/psum | solution.py:27
  273.2 1.8 convolution_convert_fusion
  274.9 0.6 copy.40
  276.5 27.4 %all_to_all.65 = bf16[16,512,64]{1,2,0:T(8,128)(2,1)S(1)} all-to-all(bf16[16,512,64]{1,2,0:T(8,128)(2,1)S(1)} %copy.41), channel_id=1, replica_groups=mesh['groups'=2,'dp'=16] {'dp'}, dimensions={0} | all-to-all | bytes 2097152 | tf_op jit(solution)/shard_map/all_to_all | solution.py:32
  304.2 1.9 copy.42
  306.1 10.6 %add_convert_fusion = bf16[512,1024]{1,0:T(8,128)(2,1)} fusion(f32[512,1024]{1,0:T(8,128)} %copy.42, bf16[512,4096]{1,0:T(8,128)(2,1)} %param.6, bf16[4096,1024]{1,0:T(8,128)(2,1)} %all-gather.2.cloned.1.call-done), kind=kOutput, calls=%fused_computation.2 | convolution fusion | flops 4296015872 | bytes 15728640 | tf_op jit(solution)/shard_map/dot_general | solution.py:13
  (15 shorter events, 2.2 us)
Async XLA Ops:
  6.5 299.6 %all-gather.2.cloned.1.call-start = ((), (), s32[]{:S(2)}) async-start(), calls=%async_computation.4 | async-start | bytes 8912896 | tf_op jit(solution)/shard_map/all_gather | solution.py:15
  9.7 18.8 %all-to-all-start.2 = ((bf16[16,2,4096]{2,1,0:T(2,128)(2,1)}), bf16[16,2,4096]{2,1,0:T(2,128)(2,1)S(1)}, u32[]{:S(2)}, u32[]{:S(2)}) async-start(bf16[16,2,4096]{2,1,0:T(2,128)(2,1)} %reshape.54), calls=%async_computation.2 | async-start | bytes 524288 | tf_op jit(solution)/shard_map/all_to_all | solution.py:21
  28.4 39.9 %all-to-all-start = ((bf16[16,2,16384]{2,1,0:T(2,128)(2,1)}), bf16[16,2,16384]{2,1,0:T(2,128)(2,1)S(1)}, u32[]{:S(2)}, u32[]{:S(2)}) async-start(bf16[16,2,16384]{2,1,0:T(2,128)(2,1)} %reshape.52), calls=%async_computation | async-start | bytes 2097152 | tf_op jit(solution)/shard_map/all_to_all | solution.py:20
  68.4 18.6 %copy-start = (s32[32]{0:T(128)S(1)}, s32[32]{0:T(128)}, u32[]{:S(2)}) copy-start(s32[32]{0:T(128)} %param.11) | copy-start | bytes 388
  68.4 18.6 %copy-start.1 = (s32[32]{0:T(128)S(1)}, s32[32]{0:T(128)}, u32[]{:S(2)}) copy-start(s32[32]{0:T(128)} %param.10) | copy-start | bytes 388
  68.4 105.6 %all-to-all-start.1 = ((bf16[512,16,256]{0,2,1:T(8,128)(2,1)}), bf16[512,16,256]{0,2,1:T(8,128)(2,1)}, u32[]{:S(2)}, u32[]{:S(2)}) async-start(bf16[512,16,256]{0,2,1:T(8,128)(2,1)} %bitcast.32), calls=%async_computation.1 | async-start | bytes 8388608 | tf_op jit(solution)/shard_map/all_to_all | solution.py:24
Sparse Core Ops, SparseCore 0:
  9.5 120.5 all-gather.1
where the time goes:
time: 325 us; the launch traced here: 324 us
  blocking collectives  117 us (36%)
  waiting for transfers between devices  112 us (34%)
  starting transfers between devices  33 us (10%)
  local copies, waits for them, and re-layouts  31.4 us (10%)
  matrix products  16 us (5%)
  between operations  13.5 us (4%)
    psum x1, blocking collectives, shards(): shrunk = lax.psum(partial_value, 'dp').astype(jnp.bfloat16)  89.3 us
    all_to_all x1, waiting for transfers between devices, shards(): lax.all_to_all(tokens, 'dp', split_axis=1, concat_axis=0, tiled=True)  81.3 us
    all_to_all x1, blocking collectives, shards(): lax.all_to_all(term_blocks, 'dp', split_axis=0, concat_axis=1, tiled=True)  27.4 us
    all_to_all x1, waiting for transfers between devices, shards(): lax.all_to_all(shrink_store, 'dp', split_axis=1, concat_axis=0, tiled=True)  26.4 us
    all_to_all x1, starting transfers between devices, shards(): lax.all_to_all(tokens, 'dp', split_axis=1, concat_axis=0, tiled=True)  18.6 us
    unnamed x11, local copies, waits for them, and re-layouts  17.9 us
    dot_general x1, matrix products, shards(): jnp.dot(tokens, lax.all_gather(base_weight, 'dp', axis=0, tiled=True), pr...  10.6 us
    all_to_all x1, starting transfers between devices, shards(): lax.all_to_all(expand_store, 'dp', split_axis=2, concat_axis=0, tiled=True)  7.39 us
  transfers between devices with their start and end apart: 4, of which 3 were waited for; matrix products, arithmetic and copies ran while one was open for 11% of the time, Pallas kernels for 0%

commit v1 on v0

v1 whole, which is shorter than its diff:
```python
import jax
import jax.numpy as jnp
from jax import lax
from jax.sharding import PartitionSpec as P


def routed_by_collectives(tokens, base_weight, shrink_store, expand_store, request_adapter, adapter_slot):
    dp_count = lax.axis_size("dp")
    slots, width, rank = shrink_store.shape
    outs = expand_store.shape[2]
    requests = request_adapter.shape[0]
    own = requests // dp_count
    gathered = lax.all_gather(base_weight, "dp", axis=0, tiled=True)
    slot_ids = adapter_slot[request_adapter]
    shares = jnp.concatenate(
        [
            shrink_store.reshape(slots, dp_count, -1),
            expand_store.reshape(slots, dp_count, -1),
        ],
        axis=2,
    )
    held = lax.all_to_all(shares, "dp", split_axis=1, concat_axis=0, tiled=True)
    picked = jnp.take(held, slot_ids, axis=0)
    mine = lax.all_to_all(picked, "dp", split_axis=0, concat_axis=1, tiled=True)
    cut = width * rank // dp_count
    down = mine[:, :, :cut].reshape(own, width, rank)
    up = mine[:, :, cut:].reshape(own, rank, outs)
    grouped = tokens.reshape(own, -1, width)
    shrunk = jnp.einsum("qsd,qdr->qsr", grouped, down, preferred_element_type=jnp.float32).astype(jnp.bfloat16)
    low_rank = jnp.einsum("qsr,qrc->qsc", shrunk, up, preferred_element_type=jnp.float32).astype(jnp.bfloat16)
    base_out = jnp.dot(tokens, gathered, preferred_element_type=jnp.float32)
    low_rank = low_rank.reshape(base_out.shape)
    return (base_out + low_rank.astype(jnp.float32)).astype(jnp.bfloat16)


def solution(mesh):
    return jax.shard_map(
        routed_by_collectives,
        mesh=mesh,
        in_specs=(
            P(("groups", "dp"), None),
            P("dp", None),
            P("dp", None, None),
            P("dp", None, None),
            P("groups"),
            P(),
        ),
        out_specs=P(("groups", "dp"), None),
        check_vma=False,
    )
```

time: 325 us -> 175 us (0.54)
  waiting for transfers between devices: 112 us -> 43.7 us
  blocking collectives: 117 us -> 62.9 us
  starting transfers between devices: 33 us -> 7.39 us
  other arithmetic: 0.47 us -> 11.4 us
  local copies, waits for them, and re-layouts: 31.4 us -> 21.2 us
    psum x1 -> x0, blocking collectives: 89.3 us -> none  [shards(): shrunk = lax.psum(partial_value, 'dp').astype(jnp.bfloat16)]
    all_to_all x3 -> x1, waiting for transfers between devices: 112 us -> 42.9 us  [routed_by_collectives(): held = lax.all_to_all(shares, 'dp', split_axis=1, concat_axis=0, tiled=True)]
    all_to_all x1, blocking collectives: 27.4 us -> 62.9 us  [routed_by_collectives(): mine = lax.all_to_all(picked, 'dp', split_axis=0, concat_axis=1, tiled=True)]
    all_to_all x3 -> x1, starting transfers between devices: 33 us -> 7.39 us  [routed_by_collectives(): held = lax.all_to_all(shares, 'dp', split_axis=1, concat_axis=0, tiled=True)]
    unnamed x11 -> x9, local copies, waits for them, and re-layouts: 17.9 us -> 7.42 us
    all_to_all x0 -> x1, other arithmetic: none -> 9.45 us  [routed_by_collectives(): mine = lax.all_to_all(picked, 'dp', split_axis=0, concat_axis=1, tiled=True)]
    all_to_all x5 -> x2, local copies, waits for them, and re-layouts: 9.01 us -> 2.46 us  [the longest x1 1.95 us: routed_by_collectives(): mine = lax.all_to_all(picked, 'dp', split_axis=0, concat_axis=1, tiled=True)]
    reshape x0 -> x4, local copies, waits for them, and re-layouts: none -> 4.55 us  [the longest x1 2.51 us: routed_by_collectives(): down = mine[:, :, :cut].reshape(own, width, rank)]
  transfers between devices with their start and end apart: 4 -> 2, of which waited for: 3 -> 1; matrix products, arithmetic and copies ran while one was open for 11% -> 20% of each run, Pallas kernels for 0% -> 0%
where the time goes in v1:
time: 175 us; the launch traced here: 174 us
  blocking collectives  62.9 us (36%)
  waiting for transfers between devices  43.7 us (25%)
  local copies, waits for them, and re-layouts  21.2 us (12%)
  matrix products  14.1 us (8%)
  between operations  13.6 us (8%)
  other arithmetic  11.4 us (7%)
  starting transfers between devices  7.39 us (4%)
    all_to_all x1, blocking collectives, routed_by_collectives(): mine = lax.all_to_all(picked, 'dp', split_axis=0, concat_axis=1, tiled=True)  62.9 us
    all_to_all x1, waiting for transfers between devices, routed_by_collectives(): held = lax.all_to_all(shares, 'dp', split_axis=1, concat_axis=0, tiled=True)  42.9 us
    dot_general x1, matrix products, routed_by_collectives(): base_out = jnp.dot(tokens, gathered, preferred_element_type=jnp.float32)  10.1 us
    all_to_all x1, other arithmetic, routed_by_collectives(): mine = lax.all_to_all(picked, 'dp', split_axis=0, concat_axis=1, tiled=True)  9.45 us
    unnamed x9, local copies, waits for them, and re-layouts  7.42 us
    all_to_all x1, starting transfers between devices, routed_by_collectives(): held = lax.all_to_all(shares, 'dp', split_axis=1, concat_axis=0, tiled=True)  7.39 us
    dot_general x1, matrix products, routed_by_collectives(): jnp.einsum('qsr,qrc->qsc', shrunk, up, preferred_element_type=jnp.float32)  3.94 us
  transfers between devices with their start and end apart: 2, of which 1 were waited for; matrix products, arithmetic and copies ran while one was open for 20% of the time, Pallas kernels for 0%

profile of v1, /device:TPU:0, one launch (start us, length us, event | category | flops | bytes accessed | tf_op | source)
XLA Modules:
  0.0 174.3 jit_solution(7150242916725068024)
XLA Ops:
  6.5 0.7 all-gather.2.cloned.1.call-update
  7.3 2.0 %copy.17 = bf16[2,4096,64]{2,1,0:T(8,128)(2,1)S(1)} copy(bf16[2,4096,64]{1,2,0:T(8,128)(2,1)} %param.8) | data formatting | bytes 2097152 | tf_op args[2]
  9.3 1.7 reshape.60
  11.3 2.5 %copy.18 = bf16[2,16,20480]{2,0,1:T(2,128)(2,1)} copy(bf16[2,16,20480]{2,1,0:T(8,128)(2,1)S(1)} %pad_maximum_fusion) | data formatting | bytes 2621440 | tf_op jit(solution)/shard_map/concatenate | solution.py:15
  13.8 7.4 %all-to-all-start = ((bf16[2,16,20480]{2,0,1:T(2,128)(2,1)}), bf16[2,16,20480]{2,0,1:T(2,128)(2,1)S(1)}, u32[]{:S(2)}, u32[]{:S(2)}) async-start(bf16[2,16,20480]{2,0,1:T(2,128)(2,1)} %copy.18), calls=%async_computation | async-start | bytes 2621440 | tf_op jit(solution)/shard_map/all_to_all | solution.py:22
  21.2 0.7 gather_fusion
  22.0 42.9 %all-to-all-done = bf16[2,16,20480]{2,0,1:T(2,128)(2,1)S(1)} async-done(((bf16[2,16,20480]{2,0,1:T(2,128)(2,1)}), bf16[2,16,20480]{2,0,1:T(2,128)(2,1)S(1)}, u32[]{:S(2)}, u32[]{:S(2)}) %all-to-all-start) | async-done | bytes 1310752 | tf_op jit(solution)/shard_map/all_to_all | solution.py:22
  64.9 0.5 reshape.74
  65.4 1.4 gather_fusion.1
  66.8 0.2 bitcast_select_fusion
  67.0 0.5 broadcast.57
  67.5 1.7 reduce.1
  69.2 0.9 reshape.87
  70.1 62.9 %all_to_all.36 = bf16[16,2,20480]{2,1,0:T(2,128)(2,1)} all-to-all(bf16[16,2,20480]{2,1,0:T(2,128)(2,1)S(1)} %reshape.87), channel_id=1, replica_groups=mesh['groups'=2,'dp'=16] {'dp'}, dimensions={0} | all-to-all | bytes 2621440 | tf_op jit(solution)/shard_map/all_to_all | solution.py:24
  133.0 4.5 %reshape.88 = bf16[32,1,20480]{2,1,0:T(2,128)(2,1)S(1)} reshape(bf16[16,2,20480]{2,1,0:T(2,128)(2,1)} %all_to_all.36) | data formatting | bytes 2621440
  137.5 9.4 %reduce = bf16[32,20480]{1,0:T(8,128)(2,1)} reduce(bf16[32,1,20480]{2,1,0:T(2,128)(2,1)S(1)} %reshape.88, bf16[]{:T(256)} %constant.20), dimensions={1}, to_apply=%all_to_all.30.reduce_sub_computation | reduce | bytes 2621442 | tf_op jit(solution)/shard_map/all_to_all | solution.py:24
  146.9 1.9 %all_to_all.31 = bf16[16,2,1,20480]{3,1,0,2:T(2,128)(2,1)S(1)} reshape(bf16[32,20480]{1,0:T(8,128)(2,1)} %reduce) | data formatting | bytes 2621440 | tf_op jit(solution)/shard_map/all_to_all | solution.py:24
  148.9 0.8 slice.12
  149.7 0.2 slice.13
  149.9 0.6 copy.20
  150.5 2.5 %reshape.62 = bf16[2,4096,64]{2,1,0:T(8,128)(2,1)S(1)} reshape(bf16[2,16,16384]{2,1,0:T(8,128)(2,1)S(1)} %copy.20) | data formatting | bytes 2097152 | tf_op jit(solution)/shard_map/reshape | solution.py:26
  153.1 0.2 reshape.64
  153.3 3.9 %convolution_convert_fusion = bf16[2,256,1024]{2,1,0:T(8,128)(2,1)S(1)} fusion(bf16[2,64,1024]{2,1,0:T(8,128)(2,1)S(1)} %reshape.64, bf16[2,4096,64]{2,1,0:T(8,128)(2,1)S(1)} %reshape.62, bf16[2,256,4096]{2,1,0:T(8,128)(2,1)} %bitcast.25), kind=kOutput, calls=%fused_computation.4 | convolution fusion | flops 336101376 | bytes 6553600 | tf_op jit(solution)/shard_map/qsr,qrc->qsc/dot_general | solution.py:30
  157.3 10.1 %fusion = bf16[512,1024]{1,0:T(8,128)(2,1)} fusion(bf16[512,1024]{1,0:T(8,128)(2,1)S(1)} %bitcast.26, bf16[512,4096]{1,0:T(8,128)(2,1)} %param.6, bf16[4096,1024]{1,0:T(8,128)(2,1)} %all-gather.2.cloned.1.call-done), kind=kOutput, calls=%fused_computation.3 | convolution fusion | flops 4296540160 | bytes 14680064 | tf_op jit(solution)/shard_map/dot_general | solution.py:31
  (16 shorter events, 0.5 us)
Async XLA Ops:
  6.5 14.7 %copy-start = (s32[32]{0:T(128)S(1)}, s32[32]{0:T(128)}, u32[]{:S(2)}) copy-start(s32[32]{0:T(128)} %param.11) | copy-start | bytes 388
  6.5 150.7 %all-gather.2.cloned.1.call-start = ((), (), s32[]{:S(2)}) async-start(), calls=%async_computation.2 | async-start | bytes 8912896 | tf_op jit(solution)/shard_map/all_gather | solution.py:13
  9.3 1.7 copy-start.1
  11.3 9.9 %copy-start.2 = (s32[32]{0:T(128)S(1)}, s32[32]{0:T(128)}, u32[]{:S(2)}) copy-start(s32[32]{0:T(128)} %param.10) | copy-start | bytes 388
  13.8 51.1 %all-to-all-start = ((bf16[2,16,20480]{2,0,1:T(2,128)(2,1)}), bf16[2,16,20480]{2,0,1:T(2,128)(2,1)S(1)}, u32[]{:S(2)}, u32[]{:S(2)}) async-start(bf16[2,16,20480]{2,0,1:T(2,128)(2,1)} %copy.18), calls=%async_computation | async-start | bytes 2621440 | tf_op jit(solution)/shard_map/all_to_all | solution.py:22
Sparse Core Ops, SparseCore 0:
  9.5 123.3 all-gather.1

commit v2 on v1

--- a/solution.py
+++ b/solution.py
@@ -1,7 +1,297 @@
 import jax
 import jax.numpy as jnp
 from jax import lax
+from jax.experimental import pallas as pl
+from jax.experimental.pallas import tpu as pltpu
 from jax.sharding import PartitionSpec as P
+
+MESH = pl.DeviceIdType.MESH
+LANES = 128
+TILE = 16
+LAYERS = 4
+CORE0, Z, Y, X, DY, DX, DX0, CZ, CY, CX, CD = 0, 0, 4, 7, 10, 13, 17, 17, 21, 24, 28
+MESSAGES = 32
+
+
+def prefill_kernel(
+    request_ref, adapter_slot, tok_hbm, w_hbm, shrink, expand, out_ref,
+    weight, tok, total, shares, held, picks, mine, ids_in, ids,
+    local_sem, base_send, base_recv, one_send, one_recv, two_send, two_recv, ids_send, ids_recv,
+):
+    gx, dp = lax.axis_index("groups"), lax.axis_index("dp")
+    groups, dp_count = lax.axis_size("groups"), lax.axis_size("dp")
+    devices = groups * dp_count
+    me = gx * dp_count + dp
+    core = dp % 2
+    y = (dp // 2) % 2
+    z = dp // 4
+    shard = w_hbm.shape[0]
+    piece = shard // 2
+    half = piece // 2
+    width = tok_hbm.shape[1]
+    deep = width // 2 // devices
+    own = mine.shape[0]
+    layers = [z, z + 1 - 2 * (z % 2), (z + 2) % LAYERS, LAYERS - 1 - z]
+
+    barrier = pltpu.get_barrier_semaphore()
+
+    def greet(i, _):
+        other = (me + i) % devices
+        pl.semaphore_signal(
+            barrier, inc=1, device_id=(other // dp_count, other % dp_count), device_id_type=MESH
+        )
+        return 0
+
+    lax.fori_loop(1, devices, greet, 0)
+    load_tok = pltpu.make_async_copy(tok_hbm, tok, local_sem.at[0])
+    load_tok.start()
+    load_w = pltpu.make_async_copy(
+        w_hbm, weight.at[pl.ds(pl.multiple_of(dp * shard, shard), shard)], local_sem.at[1]
+    )
+    load_w.start()
+
+    share_first = gx * dp_count
+
+    def pack(i, _):
+        k = share_first + i
+        low = pl.multiple_of(k * deep, TILE)
+        high = pl.multiple_of(width // 2 + k * deep, TILE)
+        row = pl.multiple_of((k // 8) * TILE, TILE)
+        col = pl.multiple_of((k % 8) * LANES, LANES)
+        for s in range(shrink.shape[0]):
+            shares[i, s, :deep, :] = jnp.concatenate(
+                [shrink[s, pl.ds(low, deep), :], shrink[s, pl.ds(high, deep), :]], axis=1
+            )
+            shares[i, s, deep:, :] = expand[s, pl.ds(row, TILE), pl.ds(col, LANES)]
+        return 0
+
+    lax.fori_loop(0, dp_count, pack, 0)
+    pl.semaphore_wait(barrier, devices - 1)
+
+    def rows_of(layer, of_x, of_y, first=0, count=piece):
+        owner = (layer * 2 + of_y) * 2 + core
+        return pl.ds(pl.multiple_of(owner * shard + of_x * piece + first, TILE), count)
+
+    def rows_of_other(layer, of_x, of_y, count=piece):
+        owner = (layer * 2 + of_y) * 2 + 1 - core
+        return pl.ds(pl.multiple_of(owner * shard + of_x * piece, TILE), count)
+
+    def message(number, src, rows, target):
+        return pltpu.make_async_remote_copy(
+            src_ref=src, dst_ref=weight.at[rows],
+            send_sem=base_send.at[number], recv_sem=base_recv.at[number],
+            device_id=target, device_id_type=MESH,
+        )
+
+    sent = []
+
+    def send(number, rows, target, src=None):
+        copy = message(number, weight.at[rows] if src is None else src, rows, target)
+        copy.start()
+        sent.append(copy)
+
+    def landed(number, rows):
+        message(number, weight.at[rows], rows, other_core).wait_recv()
+
+    fx, fy = 1 - gx, 1 - y
+    other_core = (gx, dp + 1 - 2 * core)
+    x_peer = (fx, dp)
+    y_peer = (gx, dp + 2 - 4 * y)
+    own_piece = w_hbm.at[pl.ds(pl.multiple_of(gx * piece, TILE), piece)]
+
+    swap_ids = pltpu.make_async_remote_copy(
+        src_ref=request_ref, dst_ref=ids_in, send_sem=ids_send, recv_sem=ids_recv,
+        device_id=x_peer, device_id_type=MESH,
+    )
+    swap_ids.start()
+    for i in range(1, LAYERS):
+        send(Z + i, rows_of(z, gx, y), (gx, (layers[i] * 2 + y) * 2 + core), own_piece)
+    send(Y, rows_of(z, gx, y), y_peer, own_piece)
+    send(CORE0, rows_of(z, 0, y, count=shard), other_core, w_hbm)
+
+    def share_copy(i, to, owner):
+        return pltpu.make_async_remote_copy(
+            src_ref=shares.at[to], dst_ref=held.at[pl.ds(owner * shrink.shape[0], shrink.shape[0])],
+            send_sem=one_send.at[i], recv_sem=one_recv.at[i],
+            device_id=(gx, to), device_id_type=MESH,
+        )
+
+    def send_share(i, _):
+        share_copy(i, (dp + i) % dp_count, dp).start()
+        return 0
+
+    lax.fori_loop(1, dp_count, send_share, 0)
+    held[pl.ds(dp * shrink.shape[0], shrink.shape[0])] = shares[dp]
+
+    own_ids = pltpu.make_async_copy(request_ref, ids.at[gx], local_sem.at[2])
+    own_ids.start()
+    swap_ids.wait_recv()
+    their_ids = pltpu.make_async_copy(ids_in, ids.at[fx], local_sem.at[3])
+    their_ids.start()
+    own_ids.wait()
+    their_ids.wait()
+
+    landed(Y, rows_of(z, gx, fy))
+    send(DX0, rows_of(z, gx, fy), x_peer)
+    send(CY, rows_of(z, gx, fy), other_core)
+    for i in range(1, LAYERS):
+        rows = rows_of(layers[i], gx, y)
+        landed(Z + i, rows)
+        send(Y + i, rows, y_peer)
+        send(X + i, rows, x_peer)
+        send(CZ + i, rows, other_core)
+
+    def wait_share(i, _):
+        share_copy(i, dp, (dp + dp_count - i) % dp_count).wait_recv()
+        return 0
+
+    lax.fori_loop(1, dp_count, wait_share, 0)
+
+    def pick_copy(i, to, holder):
+        return pltpu.make_async_remote_copy(
+            src_ref=picks.at[to], dst_ref=mine.at[:, holder],
+            send_sem=two_send.at[i], recv_sem=two_recv.at[i],
+            device_id=(to // dp_count, to % dp_count), device_id_type=MESH,
+        )
+
+    def pick(to, j):
+        return held[adapter_slot[ids[to // dp_count, 0, (to % dp_count) * own + j]]]
+
+    def send_pick(i, _):
+        to = (me + i) % devices
+        for j in range(own):
+            picks[to, j] = pick(to, j)
+        pick_copy(i, to, me).start()
+        return 0
+
+    lax.fori_loop(1, devices, send_pick, 0)
+    for j in range(own):
+        mine[j, me] = pick(me, j)
+
+    for i in range(1, LAYERS):
+        rows = rows_of(layers[i], fx, y)
+        landed(X + i, rows)
+        send(DY + i, rows_of(layers[i], fx, y, 0, half), y_peer)
+        send(CX + i, rows, other_core)
+        rows = rows_of(layers[i], gx, fy)
+        landed(Y + i, rows)
+        send(DX + i, rows_of(layers[i], gx, fy, half, half), x_peer)
+        send(CY + i, rows, other_core)
+    rows = rows_of(z, fx, fy)
+    landed(DX0, rows)
+    send(CD, rows, other_core)
+    for i in range(1, LAYERS):
+        landed(DY + i, rows_of(layers[i], fx, fy, 0, half))
+        landed(DX + i, rows_of(layers[i], fx, fy, half, half))
+        send(CD + i, rows_of(layers[i], fx, fy), other_core)
+
+    load_tok.wait()
+    load_w.wait()
+    block = 4 * shard
+    column = 256
+    for i in range(LAYERS):
+        layer = layers[i]
+        if i == 0:
+            landed(CORE0, rows_of_other(z, 0, y, count=shard))
+        else:
+            landed(CZ + i, rows_of_other(layer, gx, y))
+            landed(CX + i, rows_of_other(layer, fx, y))
+        landed(CY + i, rows_of_other(layer, gx, fy))
+        landed(CD + i, rows_of_other(layer, fx, fy))
+        place = pl.ds(pl.multiple_of(layer * block, block), block)
+
+        def add(n, _):
+            cols = pl.ds(pl.multiple_of(n * column, column), column)
+            term = jnp.dot(tok[:, place], weight[place, cols], preferred_element_type=jnp.float32)
+            total[:, cols] = term if i == 0 else total[:, cols] + term
+            return 0
+
+        lax.fori_loop(0, total.shape[1] // column, add, 0)
+
+    def wait_pick(i, _):
+        pick_copy(i, me, (me + devices - i) % devices).wait_recv()
+        return 0
+
+    lax.fori_loop(1, devices, wait_pick, 0)
+    seg = tok.shape[0] // own
+    rank = shrink.shape[2]
+    for j in range(own):
+        lines = pl.ds(j * seg, seg)
+        down = mine[j, :, :deep, :].reshape(width // 2, LANES)
+        first = jnp.dot(tok[lines, : width // 2], down, preferred_element_type=jnp.float32)
+        second = jnp.dot(tok[lines, width // 2 :], down, preferred_element_type=jnp.float32)
+        shrunk = (first + pltpu.roll(second, rank, 1))[:, :rank].astype(jnp.bfloat16)
+        up = jnp.concatenate(
+            [
+                jnp.concatenate([mine[j, r * 8 + c, deep:, :] for c in range(8)], axis=1)
+                for r in range(rank // TILE)
+            ],
+            axis=0,
+        )
+        low_rank = jnp.dot(shrunk, up, preferred_element_type=jnp.float32).astype(jnp.bfloat16)
+        out_ref[lines, :] = (total[lines, :] + low_rank.astype(jnp.float32)).astype(out_ref.dtype)
+
+    for copy in sent:
+        copy.wait_send()
+    swap_ids.wait_send()
+
+    def drain_one(i, _):
+        share_copy(i, (dp + i) % dp_count, dp).wait_send()
+        return 0
+
+    def drain_two(i, _):
+        pick_copy(i, (me + i) % devices, me).wait_send()
+        return 0
+
+    lax.fori_loop(1, dp_count, drain_one, 0)
+    lax.fori_loop(1, devices, drain_two, 0)
+
+
+def in_one_kernel(tokens, base_weight, shrink_store, expand_store, request_adapter, adapter_slot):
+    groups, dp_count = lax.axis_size("groups"), lax.axis_size("dp")
+    devices = groups * dp_count
+    rows, width = tokens.shape
+    slots, _, rank = shrink_store.shape
+    outs = base_weight.shape[1]
+    requests = request_adapter.shape[0]
+    own = requests // dp_count
+    tall = width // 2 // devices + TILE
+    bf16 = jnp.bfloat16
+    vmem = pl.BlockSpec(memory_space=pltpu.VMEM)
+    anywhere = pl.BlockSpec(memory_space=pl.ANY)
+    dma = pltpu.SemaphoreType.DMA
+    return pl.pallas_call(
+        prefill_kernel,
+        out_shape=jax.ShapeDtypeStruct((rows, outs), bf16),
+        in_specs=[vmem, pl.BlockSpec(memory_space=pltpu.SMEM), anywhere, anywhere, vmem, vmem],
+        out_specs=vmem,
+        scratch_shapes=[
+            pltpu.VMEM((width, outs), bf16),
+            pltpu.VMEM((rows, width), bf16),
+            pltpu.VMEM((rows, outs), jnp.float32),
+            pltpu.VMEM((dp_count, slots, tall, LANES), bf16),
+            pltpu.VMEM((dp_count * slots, tall, LANES), bf16),
+            pltpu.VMEM((devices, own, tall, LANES), bf16),
+            pltpu.VMEM((own, devices, tall, LANES), bf16),
+            pltpu.VMEM((1, requests), jnp.int32),
+            pltpu.SMEM((groups, 1, requests), jnp.int32),
+            dma((4,)),
+            dma((MESSAGES,)),
+            dma((MESSAGES,)),
+            dma((dp_count,)),
+            dma((dp_count,)),
+            dma((devices,)),
+            dma((devices,)),
+            dma,
+            dma,
+        ],
+        compiler_params=pltpu.CompilerParams(
+            collective_id=0, has_side_effects=True, vmem_limit_bytes=56 * 1024 * 1024
+        ),
+        cost_estimate=pl.CostEstimate(
+            flops=2 * rows * width * (outs + 2 * rank), bytes_accessed=16 * 1024 * 1024, transcendentals=0
+        ),
+    )(request_adapter.reshape(1, requests), adapter_slot, tokens, base_weight, shrink_store, expand_store)
 
 
 def routed_by_collectives(tokens, base_weight, shrink_store, expand_store, request_adapter, adapter_slot):
@@ -34,8 +324,9 @@
 
 
 def solution(mesh):
+    square = mesh.shape["groups"] == 2 and mesh.shape["dp"] == 16
     return jax.shard_map(
-        routed_by_collectives,
+        in_one_kernel if square else routed_by_collectives,
         mesh=mesh,
         in_specs=(
             P(("groups", "dp"), None),

time: 175 us -> 87.5 us (0.50)
  the two profiles are of different devices: /device:TPU:0 before, /device:TPU:13 now
where the time goes in v2:
time: 87.5 us; the launch traced here: 87.3 us
  Pallas kernels  82.3 us (94%)
  local copies, waits for them, and re-layouts  5.04 us (6%)
    pallas_call x1, Pallas kernels, in_one_kernel(): pl.pallas_call(prefill_kernel, out_shape=jax.ShapeDtypeStruct((rows, outs...  82.3 us
    unnamed x2, local copies, waits for them, and re-layouts  5.04 us

profile of v2, /device:TPU:13, one launch (start us, length us, event | category | flops | bytes accessed | tf_op | source)
XLA Modules:
  0.0 87.3 jit_solution(9907908426730058635)
XLA Ops:
  0.0 2.8 %copy.7.shrink = bf16[2,4096,64]{2,1,0:T(8,128)(2,1)} copy(bf16[2,4096,64]{1,2,0:T(8,128)(2,1)} %param.8) | data formatting | bytes 2097152 | tf_op args[2]
  2.8 82.3 %shard_map.64 = bf16[512,1024]{1,0:T(8,128)(2,1)} custom-call(s32[1,32]{1,0:T(1,128)} %bitcast.1, s32[32]{0:T(128)} %adapter_slot.1, bf16[512,4096]{1,0:T(8,128)(2,1)} %tok_hbm.1, bf16[256,1024]{1,0:T(8,128)(2,1)} %w_hbm.1, bf16[2,4096,64]{2,1,0:T(8,128)(2,1)} %copy.7.shrink, bf16[2,64,1024]{2,1,0:T(8,128)(2,1)} %expand.1), custom_call_target="tpu_custom_call" | custom-call | flops 4831838208 | bytes 16777216 | tf_op jit(solution)/shard_map/pallas_call | solution.py:263
  85.1 2.3 %copy.9 = bf16[512,1024]{1,0:T(8,128)(2,1)} copy(bf16[512,1024]{1,0:T(8,128)(2,1)} %shard_map.64) | data formatting | bytes 2097152

commit v3 on v2

--- a/solution.py
+++ b/solution.py
@@ -11,6 +11,8 @@
 LAYERS = 4
 CORE0, Z, Y, X, DY, DX, DX0, CZ, CY, CX, CD = 0, 0, 4, 7, 10, 13, 17, 17, 21, 24, 28
 MESSAGES = 32
+RELAY = 32
+SENDS = 36
 
 
 def prefill_kernel(
@@ -29,9 +31,12 @@
     piece = shard // 2
     half = piece // 2
     width = tok_hbm.shape[1]
-    deep = width // 2 // devices
+    rank = shrink.shape[1]
     own = mine.shape[0]
-    layers = [z, z + 1 - 2 * (z % 2), (z + 2) % LAYERS, LAYERS - 1 - z]
+    side = z // 2
+    inner = ((z + 1) // 2) % 2
+    near, across = z + 1 - 2 * (z % 2), LAYERS - 1 - z
+    layers = [z, near, 2 - side, 3 - 3 * side]
 
     barrier = pltpu.get_barrier_semaphore()
 
@@ -54,15 +59,12 @@
 
     def pack(i, _):
         k = share_first + i
-        low = pl.multiple_of(k * deep, TILE)
-        high = pl.multiple_of(width // 2 + k * deep, TILE)
-        row = pl.multiple_of((k // 8) * TILE, TILE)
-        col = pl.multiple_of((k % 8) * LANES, LANES)
+        col = pl.multiple_of(k * LANES, LANES)
+        up_row = pl.multiple_of((k // 8) * TILE, TILE)
+        up_col = pl.multiple_of((k % 8) * LANES, LANES)
         for s in range(shrink.shape[0]):
-            shares[i, s, :deep, :] = jnp.concatenate(
-                [shrink[s, pl.ds(low, deep), :], shrink[s, pl.ds(high, deep), :]], axis=1
-            )
-            shares[i, s, deep:, :] = expand[s, pl.ds(row, TILE), pl.ds(col, LANES)]
+            shares[i, s, :rank, :] = shrink[s, :, pl.ds(col, LANES)]
+            shares[i, s, rank:, :] = expand[s, pl.ds(up_row, TILE), pl.ds(up_col, LANES)]
         return 0
 
     lax.fori_loop(0, dp_count, pack, 0)
@@ -76,10 +78,10 @@
         owner = (layer * 2 + of_y) * 2 + 1 - core
         return pl.ds(pl.multiple_of(owner * shard + of_x * piece, TILE), count)
 
-    def message(number, src, rows, target):
+    def message(number, src, rows, target, send_number=None):
         return pltpu.make_async_remote_copy(
             src_ref=src, dst_ref=weight.at[rows],
-            send_sem=base_send.at[number], recv_sem=base_recv.at[number],
+            send_sem=base_send.at[number if send_number is None else send_number], recv_sem=base_recv.at[number],
             device_id=target, device_id_type=MESH,
         )
 
@@ -104,10 +106,17 @@
         device_id=x_peer, device_id_type=MESH,
     )
     swap_ids.start()
-    for i in range(1, LAYERS):
-        send(Z + i, rows_of(z, gx, y), (gx, (layers[i] * 2 + y) * 2 + core), own_piece)
-    send(Y, rows_of(z, gx, y), y_peer, own_piece)
-    send(CORE0, rows_of(z, 0, y, count=shard), other_core, w_hbm)
+    near_peer = (gx, (near * 2 + y) * 2 + core)
+    across_peer = (gx, (across * 2 + y) * 2 + core)
+    relays = []
+
+    def relay(number, rows, target, send_number, src=None):
+        copy = message(number, weight.at[rows] if src is None else src, rows, target, send_number)
+        relays.append(copy)
+
+        @pl.when(inner == 1)
+        def _():
+            copy.start()
 
     def share_copy(i, to, owner):
         return pltpu.make_async_remote_copy(
@@ -119,6 +128,11 @@
     def send_share(i, _):
         share_copy(i, (dp + i) % dp_count, dp).start()
         return 0
+
+    send(Z + 1, rows_of(z, gx, y), near_peer, own_piece)
+    relay(Z + 2, rows_of(z, gx, y), across_peer, RELAY, own_piece)
+    send(Y, rows_of(z, gx, y), y_peer, own_piece)
+    send(CORE0, rows_of(z, 0, y, count=shard), other_core, w_hbm)
 
     lax.fori_loop(1, dp_count, send_share, 0)
     held[pl.ds(dp * shrink.shape[0], shrink.shape[0])] = shares[dp]
@@ -131,44 +145,20 @@
     own_ids.wait()
     their_ids.wait()
 
-    landed(Y, rows_of(z, gx, fy))
-    send(DX0, rows_of(z, gx, fy), x_peer)
-    send(CY, rows_of(z, gx, fy), other_core)
-    for i in range(1, LAYERS):
+    def pass_first():
+        landed(Y, rows_of(z, gx, fy))
+        send(DX0, rows_of(z, gx, fy), x_peer)
+        send(CY, rows_of(z, gx, fy), other_core)
+
+    def pass_layer(i):
         rows = rows_of(layers[i], gx, y)
         landed(Z + i, rows)
+        relay((Z + 3, Z + 2, Z + 3)[i - 1], rows, across_peer if i == 1 else near_peer, RELAY + i)
         send(Y + i, rows, y_peer)
         send(X + i, rows, x_peer)
         send(CZ + i, rows, other_core)
 
-    def wait_share(i, _):
-        share_copy(i, dp, (dp + dp_count - i) % dp_count).wait_recv()
-        return 0
-
-    lax.fori_loop(1, dp_count, wait_share, 0)
-
-    def pick_copy(i, to, holder):
-        return pltpu.make_async_remote_copy(
-            src_ref=picks.at[to], dst_ref=mine.at[:, holder],
-            send_sem=two_send.at[i], recv_sem=two_recv.at[i],
-            device_id=(to // dp_count, to % dp_count), device_id_type=MESH,
-        )
-
-    def pick(to, j):
-        return held[adapter_slot[ids[to // dp_count, 0, (to % dp_count) * own + j]]]
-
-    def send_pick(i, _):
-        to = (me + i) % devices
-        for j in range(own):
-            picks[to, j] = pick(to, j)
-        pick_copy(i, to, me).start()
-        return 0
-
-    lax.fori_loop(1, devices, send_pick, 0)
-    for j in range(own):
-        mine[j, me] = pick(me, j)
-
-    for i in range(1, LAYERS):
+    def pass_sides(i):
         rows = rows_of(layers[i], fx, y)
         landed(X + i, rows)
         send(DY + i, rows_of(layers[i], fx, y, 0, half), y_peer)
@@ -177,19 +167,41 @@
         landed(Y + i, rows)
         send(DX + i, rows_of(layers[i], gx, fy, half, half), x_peer)
         send(CY + i, rows, other_core)
-    rows = rows_of(z, fx, fy)
-    landed(DX0, rows)
-    send(CD, rows, other_core)
-    for i in range(1, LAYERS):
-        landed(DY + i, rows_of(layers[i], fx, fy, 0, half))
-        landed(DX + i, rows_of(layers[i], fx, fy, half, half))
+
+    def pass_corner(i):
+        if i == 0:
+            landed(DX0, rows_of(z, fx, fy))
+        else:
+            landed(DY + i, rows_of(layers[i], fx, fy, 0, half))
+            landed(DX + i, rows_of(layers[i], fx, fy, half, half))
         send(CD + i, rows_of(layers[i], fx, fy), other_core)
 
-    load_tok.wait()
-    load_w.wait()
+    def wait_share(i, _):
+        share_copy(i, dp, (dp + dp_count - i) % dp_count).wait_recv()
+        return 0
+
+
+    def pick_copy(i, to, holder):
+        return pltpu.make_async_remote_copy(
+            src_ref=picks.at[to], dst_ref=mine.at[:, holder],
+            send_sem=two_send.at[i], recv_sem=two_recv.at[i],
+            device_id=(to // dp_count, to % dp_count), device_id_type=MESH,
+        )
+
+    def pick(to, j):
+        return held[adapter_slot[ids[to // dp_count, 0, (to % dp_count) * own + j]]]
+
+    def send_pick(i, _):
+        to = (me + i) % devices
+        for j in range(own):
+            picks[to, j] = pick(to, j)
+        pick_copy(i, to, me).start()
+        return 0
+
+
     block = 4 * shard
     column = 256
-    for i in range(LAYERS):
+    def multiply(i):
         layer = layers[i]
         if i == 0:
             landed(CORE0, rows_of_other(z, 0, y, count=shard))
@@ -208,31 +220,73 @@
 
         lax.fori_loop(0, total.shape[1] // column, add, 0)
 
-    def wait_pick(i, _):
-        pick_copy(i, me, (me + devices - i) % devices).wait_recv()
-        return 0
-
-    lax.fori_loop(1, devices, wait_pick, 0)
+    pass_first()
+    pass_layer(1)
+    pass_layer(2)
+    pass_sides(1)
+    pass_layer(3)
+    pass_sides(2)
+    lax.fori_loop(1, dp_count, wait_share, 0)
+    lax.fori_loop(1, devices, send_pick, 0)
+    for j in range(own):
+        mine[j, me] = pick(me, j)
+    pass_sides(3)
+    load_tok.wait()
+    load_w.wait()
+    pass_corner(0)
+    pass_corner(1)
+    multiply(0)
+    pass_corner(2)
+    multiply(1)
+    pass_corner(3)
+    multiply(2)
+    multiply(3)
     seg = tok.shape[0] // own
-    rank = shrink.shape[2]
+    per_layer = dp_count // LAYERS
+    shrunk = [jnp.zeros((seg, rank), jnp.float32) for _ in range(own)]
+    for i in range(LAYERS):
+        for g in range(groups):
+            first = g * dp_count + layers[i] * per_layer
+
+            def wait_pick(t, _):
+                holder = first + t
+
+                @pl.when(holder != me)
+                def _():
+                    pick_copy((me - holder + devices) % devices, me, holder).wait_recv()
+
+                return 0
+
+            lax.fori_loop(0, per_layer, wait_pick, 0)
+            span = pl.ds(pl.multiple_of(first * LANES, LANES), per_layer * LANES)
+            for j in range(own):
+                down = jnp.concatenate([mine[j, first + t, :rank, :] for t in range(per_layer)], axis=1)
+                shrunk[j] += lax.dot_general(
+                    tok[pl.ds(j * seg, seg), span], down, (((1,), (1,)), ((), ())),
+                    preferred_element_type=jnp.float32,
+                )
     for j in range(own):
         lines = pl.ds(j * seg, seg)
-        down = mine[j, :, :deep, :].reshape(width // 2, LANES)
-        first = jnp.dot(tok[lines, : width // 2], down, preferred_element_type=jnp.float32)
-        second = jnp.dot(tok[lines, width // 2 :], down, preferred_element_type=jnp.float32)
-        shrunk = (first + pltpu.roll(second, rank, 1))[:, :rank].astype(jnp.bfloat16)
         up = jnp.concatenate(
             [
-                jnp.concatenate([mine[j, r * 8 + c, deep:, :] for c in range(8)], axis=1)
+                jnp.concatenate([mine[j, r * 8 + c, rank:, :] for c in range(8)], axis=1)
                 for r in range(rank // TILE)
             ],
             axis=0,
         )
-        low_rank = jnp.dot(shrunk, up, preferred_element_type=jnp.float32).astype(jnp.bfloat16)
+        low_rank = jnp.dot(
+            shrunk[j].astype(jnp.bfloat16), up, preferred_element_type=jnp.float32
+        ).astype(jnp.bfloat16)
         out_ref[lines, :] = (total[lines, :] + low_rank.astype(jnp.float32)).astype(out_ref.dtype)
 
     for copy in sent:
         copy.wait_send()
+
+    @pl.when(inner == 1)
+    def _():
+        for copy in relays:
+            copy.wait_send()
+
     swap_ids.wait_send()
 
     def drain_one(i, _):
@@ -255,7 +309,7 @@
     outs = base_weight.shape[1]
     requests = request_adapter.shape[0]
     own = requests // dp_count
-    tall = width // 2 // devices + TILE
+    tall = rank + TILE
     bf16 = jnp.bfloat16
     vmem = pl.BlockSpec(memory_space=pltpu.VMEM)
     anywhere = pl.BlockSpec(memory_space=pl.ANY)
@@ -276,7 +330,7 @@
             pltpu.VMEM((1, requests), jnp.int32),
             pltpu.SMEM((groups, 1, requests), jnp.int32),
             dma((4,)),
-            dma((MESSAGES,)),
+            dma((SENDS,)),
             dma((MESSAGES,)),
             dma((dp_count,)),
             dma((dp_count,)),
@@ -291,7 +345,8 @@
         cost_estimate=pl.CostEstimate(
             flops=2 * rows * width * (outs + 2 * rank), bytes_accessed=16 * 1024 * 1024, transcendentals=0
         ),
-    )(request_adapter.reshape(1, requests), adapter_slot, tokens, base_weight, shrink_store, expand_store)
+    )(request_adapter.reshape(1, requests), adapter_slot, tokens, base_weight,
+      jnp.swapaxes(shrink_store, 1, 2), expand_store)
 
 
 def routed_by_collectives(tokens, base_weight, shrink_store, expand_store, request_adapter, adapter_slot):

time: 87.5 us -> 80.6 us (0.921)
  the two profiles are of different devices: /device:TPU:13 before, /device:TPU:0 now
where the time goes in v3:
time: 80.6 us; the launch traced here: 80.4 us
  Pallas kernels  78.1 us (97%)
  local copies, waits for them, and re-layouts  2.26 us (3%)
    pallas_call x1, Pallas kernels, in_one_kernel(): pl.pallas_call(prefill_kernel, out_shape=jax.ShapeDtypeStruct((rows, outs...  78.1 us
    unnamed x1, local copies, waits for them, and re-layouts  2.26 us

profile of v3, /device:TPU:0, one launch (start us, length us, event | category | flops | bytes accessed | tf_op | source)
XLA Modules:
  0.0 80.4 jit_solution(15122586860969748941)
XLA Ops:
  0.0 78.1 %shard_map.64 = bf16[512,1024]{1,0:T(8,128)(2,1)} custom-call(s32[1,32]{1,0:T(1,128)} %bitcast.3, s32[32]{0:T(128)} %adapter_slot.1, bf16[512,4096]{1,0:T(8,128)(2,1)} %tok_hbm.1, bf16[256,1024]{1,0:T(8,128)(2,1)} %w_hbm.1, bf16[2,64,4096]{2,1,0:T(8,128)(2,1)} %bitcast.2, bf16[2,64,1024]{2,1,0:T(8,128)(2,1)} %expand.1), custom_call_target="tpu_custom_call" | custom-call | flops 4831838208 | bytes 16777216 | tf_op jit(solution)/shard_map/pallas_call | solution.py:317
  78.1 2.3 %copy.8 = bf16[512,1024]{1,0:T(8,128)(2,1)} copy(bf16[512,1024]{1,0:T(8,128)(2,1)} %shard_map.64) | data formatting | bytes 2097152

commit v4 on v3

--- a/solution.py
+++ b/solution.py
@@ -16,9 +16,9 @@
 
 
 def prefill_kernel(
-    request_ref, adapter_slot, tok_hbm, w_hbm, shrink, expand, out_ref,
-    weight, tok, total, shares, held, picks, mine, ids_in, ids,
-    local_sem, base_send, base_recv, one_send, one_recv, two_send, two_recv, ids_send, ids_recv,
+    request_ref, adapter_slot, tok_hbm, w_hbm, shrink_hbm, expand_hbm, out_ref,
+    weight, tok, total, shrink, expand, shares, held, picks, mine, ids_in, ids,
+    local_sem, base_send, base_recv, one_send, one_recv, two_send, two_recv, ids_send, ids_recv, joined,
 ):
     gx, dp = lax.axis_index("groups"), lax.axis_index("dp")
     groups, dp_count = lax.axis_size("groups"), lax.axis_size("dp")
@@ -29,7 +29,8 @@
     z = dp // 4
     shard = w_hbm.shape[0]
     piece = shard // 2
-    half = piece // 2
+    by_y = piece * 2 // 4
+    by_x = piece - by_y
     width = tok_hbm.shape[1]
     rank = shrink.shape[1]
     own = mine.shape[0]
@@ -40,14 +41,18 @@
 
     barrier = pltpu.get_barrier_semaphore()
 
-    def greet(i, _):
-        other = (me + i) % devices
-        pl.semaphore_signal(
-            barrier, inc=1, device_id=(other // dp_count, other % dp_count), device_id_type=MESH
-        )
-        return 0
-
-    lax.fori_loop(1, devices, greet, 0)
+    near_peer = (gx, (near * 2 + y) * 2 + core)
+    across_peer = (gx, (across * 2 + y) * 2 + core)
+    other_core = (gx, dp + 1 - 2 * core)
+    x_peer = (1 - gx, dp)
+    y_peer = (gx, dp + 2 - 4 * y)
+    peers = [other_core, y_peer, x_peer, near_peer, across_peer]
+    for peer in peers:
+        pl.semaphore_signal(barrier, inc=1, device_id=peer, device_id_type=MESH)
+    load_shrink = pltpu.make_async_copy(shrink_hbm, shrink, local_sem.at[4])
+    load_shrink.start()
+    load_expand = pltpu.make_async_copy(expand_hbm, expand, local_sem.at[5])
+    load_expand.start()
     load_tok = pltpu.make_async_copy(tok_hbm, tok, local_sem.at[0])
     load_tok.start()
     load_w = pltpu.make_async_copy(
@@ -67,8 +72,7 @@
             shares[i, s, rank:, :] = expand[s, pl.ds(up_row, TILE), pl.ds(up_col, LANES)]
         return 0
 
-    lax.fori_loop(0, dp_count, pack, 0)
-    pl.semaphore_wait(barrier, devices - 1)
+    pl.semaphore_wait(barrier, len(peers))
 
     def rows_of(layer, of_x, of_y, first=0, count=piece):
         owner = (layer * 2 + of_y) * 2 + core
@@ -134,6 +138,14 @@
     send(Y, rows_of(z, gx, y), y_peer, own_piece)
     send(CORE0, rows_of(z, 0, y, count=shard), other_core, w_hbm)
 
+    pl.semaphore_signal(joined.at[0], inc=1, device_id=peers[0], device_id_type=MESH)
+    load_shrink.wait()
+    load_expand.wait()
+    lax.fori_loop(0, dp_count, pack, 0)
+    for r in range(len(peers)):
+        if r > 0:
+            pl.semaphore_signal(joined.at[r], inc=1, device_id=peers[r], device_id_type=MESH)
+        pl.semaphore_wait(joined.at[r], 1)
     lax.fori_loop(1, dp_count, send_share, 0)
     held[pl.ds(dp * shrink.shape[0], shrink.shape[0])] = shares[dp]
 
@@ -161,19 +173,19 @@
     def pass_sides(i):
         rows = rows_of(layers[i], fx, y)
         landed(X + i, rows)
-        send(DY + i, rows_of(layers[i], fx, y, 0, half), y_peer)
+        send(DY + i, rows_of(layers[i], fx, y, 0, by_y), y_peer)
         send(CX + i, rows, other_core)
         rows = rows_of(layers[i], gx, fy)
         landed(Y + i, rows)
-        send(DX + i, rows_of(layers[i], gx, fy, half, half), x_peer)
+        send(DX + i, rows_of(layers[i], gx, fy, by_y, by_x), x_peer)
         send(CY + i, rows, other_core)
 
     def pass_corner(i):
         if i == 0:
             landed(DX0, rows_of(z, fx, fy))
         else:
-            landed(DY + i, rows_of(layers[i], fx, fy, 0, half))
-            landed(DX + i, rows_of(layers[i], fx, fy, half, half))
+            landed(DY + i, rows_of(layers[i], fx, fy, 0, by_y))
+            landed(DX + i, rows_of(layers[i], fx, fy, by_y, by_x))
         send(CD + i, rows_of(layers[i], fx, fy), other_core)
 
     def wait_share(i, _):
@@ -191,8 +203,20 @@
     def pick(to, j):
         return held[adapter_slot[ids[to // dp_count, 0, (to % dp_count) * own + j]]]
 
+    members = dp_count // 2
+    seat = dp % members
+
+    def partner(i, way):
+        of_side = (side + 1 + i // dp_count) % 2
+        return ((gx + i // members) % groups) * dp_count + of_side * members + (seat + way * i + dp_count * 2) % members
+
+    def turn_of(holder):
+        same = 1 - (holder // members + side) % 2
+        away = (holder // dp_count + gx) % 2
+        return same * dp_count + away * members + (seat + members - holder % members) % members
+
     def send_pick(i, _):
-        to = (me + i) % devices
+        to = partner(i, 1)
         for j in range(own):
             picks[to, j] = pick(to, j)
         pick_copy(i, to, me).start()
@@ -227,13 +251,14 @@
     pass_layer(3)
     pass_sides(2)
     lax.fori_loop(1, dp_count, wait_share, 0)
-    lax.fori_loop(1, devices, send_pick, 0)
-    for j in range(own):
-        mine[j, me] = pick(me, j)
+    lax.fori_loop(0, dp_count, send_pick, 0)
     pass_sides(3)
     load_tok.wait()
     load_w.wait()
     pass_corner(0)
+    lax.fori_loop(dp_count + 1, devices, send_pick, 0)
+    for j in range(own):
+        mine[j, me] = pick(me, j)
     pass_corner(1)
     multiply(0)
     pass_corner(2)
@@ -253,7 +278,7 @@
 
                 @pl.when(holder != me)
                 def _():
-                    pick_copy((me - holder + devices) % devices, me, holder).wait_recv()
+                    pick_copy(turn_of(holder), me, holder).wait_recv()
 
                 return 0
 
@@ -294,11 +319,12 @@
         return 0
 
     def drain_two(i, _):
-        pick_copy(i, (me + i) % devices, me).wait_send()
+        pick_copy(i, partner(i, 1), me).wait_send()
         return 0
 
     lax.fori_loop(1, dp_count, drain_one, 0)
-    lax.fori_loop(1, devices, drain_two, 0)
+    lax.fori_loop(0, dp_count, drain_two, 0)
+    lax.fori_loop(dp_count + 1, devices, drain_two, 0)
 
 
 def in_one_kernel(tokens, base_weight, shrink_store, expand_store, request_adapter, adapter_slot):
@@ -317,19 +343,21 @@
     return pl.pallas_call(
         prefill_kernel,
         out_shape=jax.ShapeDtypeStruct((rows, outs), bf16),
-        in_specs=[vmem, pl.BlockSpec(memory_space=pltpu.SMEM), anywhere, anywhere, vmem, vmem],
+        in_specs=[vmem, pl.BlockSpec(memory_space=pltpu.SMEM), anywhere, anywhere, anywhere, anywhere],
         out_specs=vmem,
         scratch_shapes=[
             pltpu.VMEM((width, outs), bf16),
             pltpu.VMEM((rows, width), bf16),
             pltpu.VMEM((rows, outs), jnp.float32),
+            pltpu.VMEM((slots, rank, width), bf16),
+            pltpu.VMEM((slots, rank, outs), bf16),
             pltpu.VMEM((dp_count, slots, tall, LANES), bf16),
             pltpu.VMEM((dp_count * slots, tall, LANES), bf16),
             pltpu.VMEM((devices, own, tall, LANES), bf16),
             pltpu.VMEM((own, devices, tall, LANES), bf16),
             pltpu.VMEM((1, requests), jnp.int32),
             pltpu.SMEM((groups, 1, requests), jnp.int32),
-            dma((4,)),
+            dma((6,)),
             dma((SENDS,)),
             dma((MESSAGES,)),
             dma((dp_count,)),
@@ -338,6 +366,7 @@
             dma((devices,)),
             dma,
             dma,
+            pltpu.SemaphoreType.REGULAR((5,)),
         ],
         compiler_params=pltpu.CompilerParams(
             collective_id=0, has_side_effects=True, vmem_limit_bytes=56 * 1024 * 1024

time: 80.6 us -> 78.3 us (0.971)
  Pallas kernels: 78.1 us -> 75.8 us
    pallas_call x1, Pallas kernels: 78.1 us -> 75.8 us  [in_one_kernel(): pl.pallas_call(prefill_kernel, out_shape=jax.ShapeDtypeStruct((rows, outs...]
where the time goes in v4:
time: 78.3 us; the launch traced here: 78.1 us
  Pallas kernels  75.8 us (97%)
  local copies, waits for them, and re-layouts  2.26 us (3%)
    pallas_call x1, Pallas kernels, in_one_kernel(): pl.pallas_call(prefill_kernel, out_shape=jax.ShapeDtypeStruct((rows, outs...  75.8 us
    unnamed x1, local copies, waits for them, and re-layouts  2.26 us

profile of v4, /device:TPU:0, one launch (start us, length us, event | category | flops | bytes accessed | tf_op | source)
XLA Modules:
  0.0 78.1 jit_solution(6407539924025322561)
XLA Ops:
  0.0 75.8 %shard_map.64 = bf16[512,1024]{1,0:T(8,128)(2,1)} custom-call(s32[1,32]{1,0:T(1,128)} %bitcast.3, s32[32]{0:T(128)} %adapter_slot.1, bf16[512,4096]{1,0:T(8,128)(2,1)} %tok_hbm.1, bf16[256,1024]{1,0:T(8,128)(2,1)} %w_hbm.1, bf16[2,64,4096]{2,1,0:T(8,128)(2,1)} %bitcast.2, bf16[2,64,1024]{2,1,0:T(8,128)(2,1)} %expand_hbm.1), custom_call_target="tpu_custom_call" | custom-call | flops 4831838208 | bytes 16777216 | tf_op jit(solution)/shard_map/pallas_call | solution.py:343
  75.8 2.3 %copy.8 = bf16[512,1024]{1,0:T(8,128)(2,1)} copy(bf16[512,1024]{1,0:T(8,128)(2,1)} %shard_map.64) | data formatting | bytes 2097152

commit v5 on v4

--- a/solution.py
+++ b/solution.py
@@ -250,16 +250,16 @@
     pass_sides(1)
     pass_layer(3)
     pass_sides(2)
+    pass_sides(3)
     lax.fori_loop(1, dp_count, wait_share, 0)
     lax.fori_loop(0, dp_count, send_pick, 0)
-    pass_sides(3)
     load_tok.wait()
     load_w.wait()
     pass_corner(0)
+    pass_corner(1)
     lax.fori_loop(dp_count + 1, devices, send_pick, 0)
     for j in range(own):
         mine[j, me] = pick(me, j)
-    pass_corner(1)
     multiply(0)
     pass_corner(2)
     multiply(1)

time: 78.3 us -> 76.9 us (0.982)
  Pallas kernels: 75.8 us -> 74.5 us
    pallas_call x1, Pallas kernels: 75.8 us -> 74.5 us  [in_one_kernel(): pl.pallas_call(prefill_kernel, out_shape=jax.ShapeDtypeStruct((rows, outs...]
where the time goes in v5:
time: 76.9 us; the launch traced here: 76.8 us
  Pallas kernels  74.5 us (97%)
  local copies, waits for them, and re-layouts  2.26 us (3%)
    pallas_call x1, Pallas kernels, in_one_kernel(): pl.pallas_call(prefill_kernel, out_shape=jax.ShapeDtypeStruct((rows, outs...  74.5 us
    unnamed x1, local copies, waits for them, and re-layouts  2.26 us

profile of v5, /device:TPU:0, one launch (start us, length us, event | category | flops | bytes accessed | tf_op | source)
XLA Modules:
  0.0 76.8 jit_solution(14961938688938722156)
XLA Ops:
  0.0 74.5 %shard_map.64 = bf16[512,1024]{1,0:T(8,128)(2,1)} custom-call(s32[1,32]{1,0:T(1,128)} %bitcast.3, s32[32]{0:T(128)} %adapter_slot.1, bf16[512,4096]{1,0:T(8,128)(2,1)} %tok_hbm.1, bf16[256,1024]{1,0:T(8,128)(2,1)} %w_hbm.1, bf16[2,64,4096]{2,1,0:T(8,128)(2,1)} %bitcast.2, bf16[2,64,1024]{2,1,0:T(8,128)(2,1)} %expand_hbm.1), custom_call_target="tpu_custom_call" | custom-call | flops 4831838208 | bytes 16777216 | tf_op jit(solution)/shard_map/pallas_call | solution.py:343
  74.5 2.3 %copy.8 = bf16[512,1024]{1,0:T(8,128)(2,1)} copy(bf16[512,1024]{1,0:T(8,128)(2,1)} %shard_map.64) | data formatting | bytes 2097152
